TPU v7x, 128 devices: a whole 4x4x4 slice. The times are simulated.
128 devices in a mesh: row: 4 (over z), col: 32 (over x, y, core).
Axes of the slice: x: 4, y: 4, z: 4, core: 2. Of those that a mesh axis runs over, the one named last changes fastest.
Arguments:
- splat_params: float32 [10, 8388608], P(None, ('row', 'col')), as said below
- list_owner: int32 [512, 1024, 1], P(('row', 'col')), may hold values from 0 to 127; in each aligned block of 4096 rows (0 to 4095, 4096 to 8191, ..., all dimensions but the last counted through in order) at most 64 rows name the same one
- list_slot: int32 [512, 1024], P(('row', 'col')), may hold values from 0 to 65535
- list_length: int32 [512], P(('row', 'col')), may hold values from 512 to 1024, as said below
- target: float32 [4, 512, 256], P(None, ('row', 'col')), may hold values from 0 to 1
Outputs:
- rendered: float32 [4, 512, 256], P(None, ('row', 'col'))
- splat_grads: float32 [10, 8388608], P(None, ('row', 'col'))
Inputs may be any that keep to these rules, and one draw needn't show every extreme that they name: `list_owner`: within the entries of one device's tiles (aligned blocks of 4096 entries), no owner is named more than 64 times, a bound that some block reaches. `list_length`: some tile has exactly 1024 live entries; every tile has at least 512. `splat_params`: conic entries satisfy a > 0, c > 0 and b * b < a * c; opacity lies in (0, 0.02]; colours and depth lie in [0, 1].
All inputs are finite; a program needn't handle non-finite values.
Results may differ from a plain program's by a relative error of at most 0.0003.
Values sent between devices are 32-bit elements; how exact they have to be, the bound alone decides.
No kernel may reach another device: no remote copies, remote signals or barrier semaphores. Data moves between devices by JAX's collectives and lax.ppermute only.
A program may use at most 128 MiB of HBM per device.

v0:
```python
import jax
import jax.numpy as jnp
from jax import lax
from jax.sharding import PartitionSpec as P

SIDE = 16
SB = 256


precise = lax.Precision.HIGHEST


def render_tile(values, tile_target):
    pixel_count = tile_target.shape[1]
    pixel_index = jnp.arange(pixel_count)
    pixel_x = (pixel_index % SIDE).astype(jnp.float32) + 0.5
    pixel_y = (pixel_index // SIDE).astype(jnp.float32) + 0.5
    live_count = jnp.sum((values[5] > 0.0).astype(jnp.int32))
    blocks = (live_count + SB - 1) // SB
    block_index = jnp.arange(SB)
    strict = (block_index[:, None] < block_index[None, :]).astype(jnp.float32)
    inclusive = (block_index[:, None] <= block_index[None, :]).astype(jnp.float32)

    def geometry(start):
        block_values = lax.dynamic_slice_in_dim(values, start, SB, 1)
        offset_x = pixel_x[:, None] - block_values[0][None, :]
        offset_y = pixel_y[:, None] - block_values[1][None, :]
        exponent = (
            0.5 * (block_values[2] * offset_x * offset_x + block_values[4] * offset_y * offset_y)
            + block_values[3] * offset_x * offset_y
        )
        falloff = jnp.exp(-exponent)
        alphas = block_values[5][None, :] * falloff
        log_keep = jnp.log1p(-alphas)
        return (block_values, offset_x, offset_y, falloff, alphas, log_keep)

    def forward(block_step, state):
        carried, rendered = state
        block_values, offset_x, offset_y, falloff, alphas, log_keep = geometry(block_step * SB)
        transmit = jnp.exp(carried[:, None] + jnp.dot(log_keep, strict, precision=precise))
        weight = alphas * transmit
        rendered = rendered + lax.dot_general(
            block_values[6:10], weight, (((1,), (1,)), ((), ())), precision=precise
        )
        return (carried + jnp.sum(log_keep, axis=1), rendered)

    start_state = (jnp.zeros((pixel_count,), jnp.float32), jnp.zeros((4, pixel_count), jnp.float32))
    carried, rendered = lax.fori_loop(0, blocks, forward, start_state)
    grad_image = 2.0 * (rendered - tile_target)
    grand_total = jnp.sum(grad_image * rendered, axis=0)

    def backward(block_step, state):
        carried, spent_before, grad_rows = state
        start = block_step * SB
        block_values, offset_x, offset_y, falloff, alphas, log_keep = geometry(start)
        transmit = jnp.exp(carried[:, None] + jnp.dot(log_keep, strict, precision=precise))
        weight = alphas * transmit
        shading = lax.dot_general(
            grad_image, block_values[6:10], (((0,), (0,)), ((), ())), precision=precise
        )
        spent_sum = weight * shading
        before = spent_before[:, None] + jnp.dot(spent_sum, inclusive, precision=precise)
        grad_alpha = transmit * shading - (grand_total[:, None] - before) / (1.0 - alphas)
        grad_power = -grad_alpha * alphas
        conic_a = block_values[2]
        conic_b = block_values[3]
        conic_c = block_values[4]
        grad_mean_x = jnp.sum(-grad_power * (conic_a * offset_x + conic_b * offset_y), axis=0)
        grad_mean_y = jnp.sum(-grad_power * (conic_c * offset_y + conic_b * offset_x), axis=0)
        grad_a = jnp.sum(grad_power * 0.5 * offset_x * offset_x, axis=0)
        grad_b = jnp.sum(grad_power * offset_x * offset_y, axis=0)
        grad_c = jnp.sum(grad_power * 0.5 * offset_y * offset_y, axis=0)
        live_mask = (block_values[5] > 0.0).astype(jnp.float32)
        grad_opacity = jnp.sum(grad_alpha * falloff, axis=0) * live_mask
        grad_colours = jnp.dot(grad_image, weight, precision=precise)
        geometry_grads = jnp.stack([grad_mean_x, grad_mean_y, grad_a, grad_b, grad_c, grad_opacity])
        update = jnp.concatenate([geometry_grads, grad_colours], axis=0)
        grad_rows = lax.dynamic_update_slice_in_dim(grad_rows, update, start, 1)
        return (
            carried + jnp.sum(log_keep, axis=1),
            spent_before + jnp.sum(spent_sum, axis=1),
            grad_rows,
        )

    back_state = (
        jnp.zeros((pixel_count,), jnp.float32),
        jnp.zeros((pixel_count,), jnp.float32),
        jnp.zeros(values.shape, jnp.float32),
    )
    finished = lax.fori_loop(0, blocks, backward, back_state)
    return (rendered, finished[2])


def render_all(values, tile_targets):
    tile_count = values.shape[1]

    def render_one(tile_step, state):
        images, grad_rows = state
        tile_values = lax.dynamic_index_in_dim(values, tile_step, 1, keepdims=False)
        tile_target = lax.dynamic_index_in_dim(tile_targets, tile_step, 1, keepdims=False)
        rendered, tile_grads = render_tile(tile_values, tile_target)
        images = lax.dynamic_update_index_in_dim(images, rendered, tile_step, 1)
        grad_rows = lax.dynamic_update_index_in_dim(grad_rows, tile_grads, tile_step, 1)
        return (images, grad_rows)

    start_state = (jnp.zeros(tile_targets.shape, jnp.float32), jnp.zeros(values.shape, jnp.float32))
    return lax.fori_loop(0, tile_count, render_one, start_state)


def body(splat_params, list_owner, list_slot, list_length, target):
    devices = lax.axis_size(("row", "col"))
    tile_count = list_slot.shape[0]
    list_count = list_slot.shape[1]
    entries = tile_count * list_count
    capacity = 2 * entries // devices
    owners = list_owner.reshape(entries)
    slot_ids = list_slot.reshape(entries)
    sort_order = jnp.argsort(owners, stable=True)
    sorted_owner = owners[sort_order]
    starts = jnp.searchsorted(sorted_owner, jnp.arange(devices, dtype=jnp.int32))
    position = jnp.arange(entries, dtype=jnp.int32) - starts[sorted_owner]
    slot_rank = jnp.zeros((entries,), jnp.int32).at[sort_order].set(position)
    requests = jnp.zeros((devices, capacity), jnp.int32).at[owners, slot_rank].set(slot_ids)
    asked_slots = lax.all_to_all(requests, ("row", "col"), split_axis=0, concat_axis=0, tiled=True)
    looked = jnp.take(splat_params, asked_slots, axis=1)
    answer = lax.all_to_all(looked, ("row", "col"), split_axis=1, concat_axis=1, tiled=True)
    replies, asked_slots = (answer, asked_slots[None])
    fetched = replies[:, owners, slot_rank].reshape(10, tile_count, list_count)
    live_mask = (jnp.arange(list_count)[None, :] < list_length[:, None]).astype(jnp.float32)
    values = jnp.concatenate([fetched[:5], fetched[5:6] * live_mask[None], fetched[6:]], axis=0)
    images, entry_grads = render_all(values, target)
    flat_grads = entry_grads.reshape(10, entries)
    outgoing = (
        jnp.zeros((10, devices, capacity), jnp.float32).at[:, owners, slot_rank].set(flat_grads)
    )
    incoming = lax.all_to_all(outgoing, ("row", "col"), split_axis=1, concat_axis=1, tiled=True)
    splat_grads = jnp.zeros(splat_params.shape, jnp.float32).at[:, asked_slots[0]].add(incoming)
    return (images, splat_grads)


def solution(mesh):
    in_specs = (
        P(None, ("row", "col")),
        P(("row", "col"), None, None),
        P(("row", "col"), None),
        P(("row", "col")),
        P(None, ("row", "col"), None),
    )
    out_specs = (P(None, ("row", "col"), None), P(None, ("row", "col")))
    return jax.shard_map(body, mesh=mesh, in_specs=in_specs, out_specs=out_specs, check_vma=False)
```

profile of v0, /device:TPU:1, one launch (start us, length us, event | category | flops | bytes accessed | tf_op | source)
XLA Modules:
  0.0 452.4 jit_solution(3506682206738903410)
XLA Ops:
  0.7 6.5 %sort.17 = (s32[4096]{0:T(1024)}, s32[4096]{0:T(1024)S(1)}) sort(s32[4096]{0:T(1024)} %bitcast.137, s32[4096]{0:T(1024)S(1)} %iota.64), dimensions={0}, to_apply=%region_0.0 | sort | flops 49152 | bytes 65536 | tf_op jit(solution)/shard_map/jit(argsort)/sort | solution.py:118
  7.2 23.0 %gather_fusion.1 = s32[4096]{0:T(1024)S(1)} fusion(s32[4096]{0:T(1024)S(1)} %bitcast.138, s32[4096]{0:T(1024)S(1)} %get-tuple-element.534), kind=kCustom, calls=%fused_computation.1 | custom fusion | bytes 49152 | tf_op jit(solution)/shard_map/gather | solution.py:119
  30.3 15.8 %while.141 = (s32[]{:T(128)}, u32[128]{0:T(128)S(1)}, u32[128]{0:T(128)S(1)}, s32[4096]{0:T(1024)S(1)}, s32[]{:T(128)}, /*index=5*/s32[]{:T(128)}, s32[]{}) while((s32[]{:T(128)}, u32[128]{0:T(128)S(1)}, u32[128]{0:T(128)S(1)}, s32[4096]{0:T(1024)S(1)}, s32[]{:T(128)}, /*index=5*/s32[]{:T(128)}, s32[]{}) %tuple.165), condition=%wide.region_2.3_spmd.clone, body=%wide.region_1.2_spmd.clone.sunk | while | flops 2692 | bytes 10340 | solution.py:120
  46.2 24.7 %gather_fusion.2 = s32[4096]{0:T(1024)S(1)} fusion(s32[128]{0:T(128)S(1)} %convert_element_type.90, s32[4096]{0:T(1024)S(1)} %broadcast_clamp_fusion.1), kind=kCustom, calls=%fused_computation.2 | custom fusion | bytes 49152 | tf_op jit(solution)/shard_map/gather | solution.py:121
  70.9 15.5 %scatter_custom_fusion = s32[4096]{0:T(1024)S(1)} fusion(s32[4096]{0:T(1024)S(1)} %get-tuple-element.535, s32[4096]{0:T(1024)S(1)} %iota_subtract_fusion, s32[]{:T(128)} %constant.288.clone.1), kind=kCustom, calls=%fused_computation.158 | custom fusion | bytes 16388 | tf_op jit(solution)/shard_map/scatter | solution.py:122
  86.8 15.5 %scatter_custom_fusion.2 = s32[8192]{0:T(1024)S(1)} fusion(s32[4096]{0:T(1024)S(1)} %broadcast_select_fusion.2, s32[4096]{0:T(1024)S(1)} %bitcast.198, s32[]{:T(128)} %constant.288.clone.1), kind=kCustom, calls=%fused_computation.150 | custom fusion | bytes 32772
  103.1 11.5 %all-to-all-start = ((s32[128,1,64]{2,1,0:T(1,128)}), s32[128,1,64]{2,1,0:T(1,128)S(1)}, u32[]{:S(2)}, u32[]{:S(2)}) async-start(s32[128,1,64]{2,1,0:T(1,128)} %copy.40), calls=%async_computation | async-start | bytes 131072 | tf_op jit(solution)/shard_map/all_to_all | solution.py:124
  114.6 16.9 %copy.41 = f32[10,65536]{0,1:T(8,128)} copy(f32[10,65536]{1,0:T(8,128)} %param.13) | data formatting | bytes 5242880 | tf_op args[0]
  131.6 38.5 %gather_fusion.3 = f32[8192,10]{1,0:T(8,128)} fusion(f32[10,65536]{0,1:T(8,128)} %copy.41, s32[8192]{0:T(1024)S(1)} %broadcast_clamp_fusion), kind=kCustom, calls=%fused_computation.3 | custom fusion | bytes 688128 | tf_op jit(solution)/shard_map/jit(_take)/gather | solution.py:125
  174.5 9.8 %all-to-all-start.1 = ((f32[128,1,640]{2,1,0:T(1,128)}), f32[128,1,640]{2,1,0:T(1,128)S(1)}, u32[]{:S(2)}, u32[]{:S(2)}) async-start(f32[128,1,640]{2,1,0:T(1,128)} %reshape.245), calls=%async_computation.1 | async-start | bytes 655360 | tf_op jit(solution)/shard_map/all_to_all | solution.py:126
  184.3 11.5 %all-to-all-done.1 = f32[128,1,640]{2,1,0:T(1,128)S(1)} async-done(((f32[128,1,640]{2,1,0:T(1,128)}), f32[128,1,640]{2,1,0:T(1,128)S(1)}, u32[]{:S(2)}, u32[]{:S(2)}) %all-to-all-start.1) | async-done | bytes 327712 | tf_op jit(solution)/shard_map/all_to_all | solution.py:126
  200.9 44.0 %gather_fusion.4 = f32[4096,10]{1,0:T(8,128)S(1)} fusion(f32[10,128,64]{0,2,1:T(8,128)} %copy.43, s32[4096]{0:T(1024)S(1)} %bitcast.141), kind=kCustom, calls=%fused_computation.4 | custom fusion | bytes 360448 | tf_op jit(solution)/shard_map/gather | solution.py:128
  251.1 63.0 %while.140 = (s32[]{:T(128)}, f32[4,4,256]{2,1,0:T(4,128)S(1)}, f32[10,4,1024]{2,1,0:T(4,128)S(1)}, f32[10,4,1024]{2,0,1:T(8,128)S(1)}, f32[4,4,256]{2,1,0:T(4,1...) while((s32[]{:T(128)}, f32[4,4,256]{2,1,0:T(4,128)S(1)}, ...), condition=%wide.region_21.22_spmd, body=%wide.region_5.21_spmd.sunk | while | flops 622607104 | bytes 2349421 | solution.py:107
  252.4 4.5 while.142
  257.7 8.0 %while.143 = (s32[]{:T(128)}, f32[256]{0:T(256)S(1)}, f32[256]{0:T(256)S(1)}, f32[10,1024]{1,0:T(8,128)S(1)}, s32[]{:T(128)}, /*index=5*/f32[10,1024]{1,0:T(8,12...) while((s32[]{:T(128)}, f32[256]{0:T(256)S(1)}, ...), condition=%wide.region_20.20_spmd.clone, body=%wide.region_11.19_spmd.clone.sunk | while | flops 415108096 | bytes 1440063 | solution.py:90
  268.2 4.5 while.142
  273.4 8.0 %while.143 = (s32[]{:T(128)}, f32[256]{0:T(256)S(1)}, f32[256]{0:T(256)S(1)}, f32[10,1024]{1,0:T(8,128)S(1)}, s32[]{:T(128)}, /*index=5*/f32[10,1024]{1,0:T(8,12...) while((s32[]{:T(128)}, f32[256]{0:T(256)S(1)}, ...), condition=%wide.region_20.20_spmd.clone, body=%wide.region_11.19_spmd.clone.sunk | while | flops 415108096 | bytes 1440063 | solution.py:90
  289.2 8.0 %while.143 = (s32[]{:T(128)}, f32[256]{0:T(256)S(1)}, f32[256]{0:T(256)S(1)}, f32[10,1024]{1,0:T(8,128)S(1)}, s32[]{:T(128)}, /*index=5*/f32[10,1024]{1,0:T(8,12...) while((s32[]{:T(128)}, f32[256]{0:T(256)S(1)}, ...), condition=%wide.region_20.20_spmd.clone, body=%wide.region_11.19_spmd.clone.sunk | while | flops 415108096 | bytes 1440063 | solution.py:90
  299.7 4.5 while.142
  304.9 8.0 %while.143 = (s32[]{:T(128)}, f32[256]{0:T(256)S(1)}, f32[256]{0:T(256)S(1)}, f32[10,1024]{1,0:T(8,128)S(1)}, s32[]{:T(128)}, /*index=5*/f32[10,1024]{1,0:T(8,12...) while((s32[]{:T(128)}, f32[256]{0:T(256)S(1)}, ...), condition=%wide.region_20.20_spmd.clone, body=%wide.region_11.19_spmd.clone.sunk | while | flops 415108096 | bytes 1440063 | solution.py:90
  314.9 12.8 %scatter_custom_fusion.3 = f32[10,8192]{0,1:T(8,128)} fusion(s32[4096]{0:T(1024)S(1)} %broadcast_select_fusion.2, f32[4096,10]{1,0:T(8,128)S(1)} %copy.49, f32[]{:T(128)} %constant.289.clone.1), kind=kCustom, calls=%fused_computation.133 | custom fusion | bytes 327684
  332.1 32.1 %all_to_all.25 = f32[128,1,640]{2,1,0:T(1,128)S(1)} all-to-all(f32[128,1,640]{2,1,0:T(1,128)S(1)} %reshape.247), channel_id=1, replica_groups=mesh['row'=4,'col'=32] {'row','col'}, dimensions={0} | all-to-all | bytes 655360 | tf_op jit(solution)/shard_map/all_to_all | solution.py:136
  368.7 64.3 %scatter_custom_fusion.1 = f32[10,65536]{0,1:T(8,128)} fusion(s32[8192]{0:T(1024)S(1)} %reshape.188, f32[8192,10]{1,0:T(8,128)} %bitcast.150, f32[]{:T(128)} %constant.289.clone.1), kind=kCustom, calls=%fused_computation.130 | custom fusion | flops 81920 | bytes 2621952 | tf_op jit(solution)/shard_map/scatter-add | solution.py:137
  433.0 19.4 %copy.54 = f32[10,65536]{1,0:T(8,128)} copy(f32[10,65536]{0,1:T(8,128)} %scatter_custom_fusion.1) | data formatting | bytes 5242880
  (368 shorter events, 104.7 us)
Async XLA Ops:
  0.6 6.6 %copy-start = (s32[4,1024,1]{1,2,0:T(1,128)S(1)}, s32[4,1024,1]{1,2,0:T(1,128)}, u32[]{:S(2)}) copy-start(s32[4,1024,1]{1,2,0:T(1,128)} %param.14) | copy-start | bytes 49156
  46.1 40.4 %copy-start.4 = (s32[2]{0:T(128)S(1)}, s32[2]{0:T(128)}, u32[]{:S(2)}) copy-start(s32[2]{0:T(128)} %constant.302) | copy-start | bytes 28
  46.1 40.5 %copy-start.3 = (s32[2]{0:T(128)S(1)}, s32[2]{0:T(128)}, u32[]{:S(2)}) copy-start(s32[2]{0:T(128)} %constant.305) | copy-start | bytes 28
  46.2 40.6 %copy-start.1 = (s32[4,1024]{1,0:T(4,128)S(1)}, s32[4,1024]{1,0:T(4,128)}, u32[]{:S(2)}) copy-start(s32[4,1024]{1,0:T(4,128)} %param.15) | copy-start | bytes 49156
  103.1 28.5 %all-to-all-start = ((s32[128,1,64]{2,1,0:T(1,128)}), s32[128,1,64]{2,1,0:T(1,128)S(1)}, u32[]{:S(2)}, u32[]{:S(2)}) async-start(s32[128,1,64]{2,1,0:T(1,128)} %copy.40), calls=%async_computation | async-start | bytes 131072 | tf_op jit(solution)/shard_map/all_to_all | solution.py:124
  174.5 21.3 %all-to-all-start.1 = ((f32[128,1,640]{2,1,0:T(1,128)}), f32[128,1,640]{2,1,0:T(1,128)S(1)}, u32[]{:S(2)}, u32[]{:S(2)}) async-start(f32[128,1,640]{2,1,0:T(1,128)} %reshape.245), calls=%async_computation.1 | async-start | bytes 655360 | tf_op jit(solution)/shard_map/all_to_all | solution.py:126
  246.8 4.0 copy-start.2
  314.1 17.5 %copy-start.5 = (f32[4,4,256]{2,1,0:T(4,128)}, f32[4,4,256]{2,1,0:T(4,128)S(1)}, u32[]{:S(2)}) copy-start(f32[4,4,256]{2,1,0:T(4,128)S(1)} %get-tuple-element.458) | copy-start | bytes 49156
where the time goes:
time: 454 us; the launch traced here: 452 us
  local copies, waits for them, and re-layouts  260 us (57%)
  other arithmetic  83 us (18%)
  matrix products  38.7 us (9%)
  blocking collectives  32.1 us (7%)
  starting transfers between devices  21.3 us (5%)
  waiting for transfers between devices  11.5 us (3%)
  loops' own time  4.97 us (1%)
    unnamed x25, local copies, waits for them, and re-layouts  70.9 us
    scatter-add x1, other arithmetic, body(): jnp.zeros(splat_params.shape, jnp.float32).at[:, asked_slots[0]]  64.3 us
    gather x1, local copies, waits for them, and re-layouts, body(): fetched = replies[:, owners, slot_rank].reshape(10, tile_count, list_count)  44 us
    gather x2, local copies, waits for them, and re-layouts, body(): looked = jnp.take(splat_params, asked_slots, axis=1)  41.5 us
    all_to_all x1, blocking collectives, body(): lax.all_to_all(outgoing, ('row', 'col'), split_axis=1, concat_axis=1, til...  32.1 us
    gather x1, local copies, waits for them, and re-layouts, body(): position = jnp.arange(entries, dtype=jnp.int32) - starts[sorted_owner]  24.7 us
    gather x1, local copies, waits for them, and re-layouts, body(): sorted_owner = owners[sort_order]  23 us
    scatter x1, local copies, waits for them, and re-layouts, body(): slot_rank = jnp.zeros((entries,), jnp.int32).at[sort_order].set(position)  15.5 us
  transfers between devices with their start and end apart: 2, of which 1 were waited for; matrix products, arithmetic and copies ran while one was open for 4% of the time, Pallas kernels for 0%

commit v1 on v0

v1 whole, which is shorter than its diff:
```python
import jax
import jax.numpy as jnp
from jax import lax
from jax.experimental import pallas as pl
from jax.experimental.pallas import tpu as pltpu
from jax.sharding import PartitionSpec as P

AXES = ("row", "col")
DEVS = 128
RANKS = 64
TILES = 4
SEGS = 128
STEPS = 8
ROWS = TILES * STEPS
WIRE = 5
LOG2E = 1.4426950408889634
F32 = jnp.float32
BF16 = jnp.bfloat16


def iota(shape, dim):
    return lax.broadcasted_iota(jnp.int32, shape, dim)


def dot(a, b):
    return lax.dot_general(a, b, (((1,), (0,)), ((), ())), preferred_element_type=F32)


def dot_nt(a, b):
    return lax.dot_general(a, b, (((1,), (1,)), ((), ())), preferred_element_type=F32)


def split(x, parts):
    out = []
    for _ in range(parts - 1):
        head = x.astype(BF16)
        out.append(head)
        x = x - head.astype(F32)
    out.append(x.astype(BF16))
    return out


def onehot_rows(row, count):
    wide = jnp.broadcast_to(row, (count, row.shape[1]))
    return wide == iota(wide.shape, 0).astype(F32)


def route_kernel(length_ref, owner_ref, slot_ref, request_ref, owner_out, rank_out):
    lane = iota((STEPS, SEGS), 1)
    step = iota((STEPS, SEGS), 0)
    picks = (lane & (STEPS - 1)) == step
    pieces = []
    for r in range(STEPS):
        rows = []
        slot_rows = []
        for t in range(TILES):
            own = jnp.broadcast_to(owner_ref[t * STEPS + r : t * STEPS + r + 1, :], (STEPS, SEGS))
            rows.append(jnp.where(picks, own, 0))
            slot = slot_ref[t : t + 1, r * SEGS : (r + 1) * SEGS]
            slot_rows.append(jnp.where(picks, jnp.broadcast_to(slot, (STEPS, SEGS)), 0))
        rows += [s >> 8 for s in slot_rows] + [s & 255 for s in slot_rows]
        pieces.append(jnp.concatenate(rows, axis=0).astype(F32).astype(BF16))
    spread = jnp.concatenate(pieces, axis=1)
    place = ((iota((STEPS * SEGS, SEGS), 0) >> 3) == iota((STEPS * SEGS, SEGS), 1)).astype(F32)
    moved = dot(spread, place.astype(BF16))
    lane = iota((ROWS, SEGS), 1)
    row = iota((ROWS, SEGS), 0)
    length = jnp.full((ROWS, SEGS), length_ref[0], jnp.int32)
    for t in range(1, TILES):
        length = jnp.where((row >> 3) == t, length_ref[t], length)
    live = (lane * STEPS + (row & (STEPS - 1))) < length
    owners = jnp.where(live, moved[0:ROWS], -1.0)
    high = moved[ROWS : 2 * ROWS]
    low = moved[2 * ROWS : 3 * ROWS]
    owner_out[...] = owners
    before = (iota((256, 256), 0) < iota((256, 256), 1)).astype(F32).astype(BF16)
    before = jnp.concatenate([before, jnp.ones((256, 256), BF16)], axis=1)
    rank_of = (iota((2 * RANKS, 256), 0) & (RANKS - 1)).astype(F32)
    upper = iota((2 * RANKS, 256), 0) < RANKS
    carry = jnp.zeros((DEVS, 256), F32)
    request = jnp.zeros((2 * RANKS, DEVS), F32)
    for n in range(ROWS // 2):
        pair = lambda x: jnp.concatenate([x[2 * n : 2 * n + 1], x[2 * n + 1 : 2 * n + 2]], axis=1)
        hot = onehot_rows(pair(owners), DEVS)
        hot16 = hot.astype(F32).astype(BF16)
        counted = dot(hot16, before)
        rank = jnp.sum(jnp.where(hot, counted[:, :256] + carry, 0.0), axis=0, keepdims=True)
        carry = carry + counted[:, 256:]
        rank_out[2 * n : 2 * n + 1, :] = rank[:, :SEGS]
        rank_out[2 * n + 1 : 2 * n + 2, :] = rank[:, SEGS:]
        values = jnp.where(upper, pair(high), pair(low))
        values = jnp.where(rank_of == rank, values, 0.0)
        request = request + dot_nt(values.astype(BF16), hot16)
    slots = request[:RANKS] * 256.0 + request[RANKS:]
    slots = jnp.concatenate([slots, slots], axis=0).T
    full = jnp.where(iota((DEVS, DEVS), 1) < RANKS, slots, carry[:, :DEVS])
    request_ref[...] = full.astype(jnp.int32)


def gather_kernel(asked_ref, params_ref, out_ref, held_ref):
    lane8 = iota((8, 128), 1)
    lane2 = iota((2, 128), 1)
    left = iota((WIRE, 128), 1) < RANKS

    def pair(j, carry):
        held_ref[...] = jnp.zeros((16, 128), F32)
        for side in range(2):
            src = 2 * j + side
            count = asked_ref[src, RANKS]
            for chunk in range(RANKS // 8):

                @pl.when(count > chunk * 8)
                def _():
                    top = jnp.zeros((8, 128), F32)
                    low = jnp.zeros((2, 128), F32)
                    for i in range(8):
                        rank = chunk * 8 + i
                        spot = side * RANKS + rank
                        slot = asked_ref[src, rank]
                        base = pl.multiple_of((slot >> 7) << 7, 128)
                        turn = (spot - slot) & 127
                        a = pltpu.roll(params_ref[0:8, pl.ds(base, 128)], turn, 1)
                        b = pltpu.roll(params_ref[8:10, pl.ds(base, 128)], turn, 1)
                        top = jnp.where(lane8 == spot, a, top)
                        low = jnp.where(lane2 == spot, b, low)
                    held_ref[0:8, :] += top
                    held_ref[8:10, :] += low

        first = held_ref[0:WIRE, :]
        second = held_ref[WIRE : 2 * WIRE, :]
        even = jnp.where(left, first, pltpu.roll(second, RANKS, 1))
        odd = jnp.where(left, pltpu.roll(first, RANKS, 1), second)
        out_ref[pl.ds(j * 2 * WIRE, 2 * WIRE), :] = jnp.concatenate([even, odd], axis=0)
        return carry

    lax.fori_loop(0, DEVS // 2, pair, 0)


CHAINS = 4


def scatter_kernel(asked_ref, wire_ref, out_ref, held_ref, *more):
    totals = (out_ref,) + more
    left = iota((WIRE, 128), 1) < RANKS
    lane8 = iota((8, 128), 1)
    lane2 = iota((2, 128), 1)
    width = 1024

    def clear(i, carry):
        at = pl.ds(pl.multiple_of(i * width, width), width)
        for ref in totals:
            ref[:, at] = jnp.zeros((10, width), F32)
        return carry

    lax.fori_loop(0, out_ref.shape[1] // width, clear, 0)

    def pair(j, carry):
        both = wire_ref[pl.ds(j * 2 * WIRE, 2 * WIRE), :]
        even = both[:WIRE]
        odd = both[WIRE:]
        held_ref[0:WIRE, :] = jnp.where(left, even, pltpu.roll(odd, RANKS, 1))
        held_ref[WIRE : 2 * WIRE, :] = jnp.where(left, pltpu.roll(even, RANKS, 1), odd)
        for side in range(2):
            src = 2 * j + side
            count = asked_ref[src, RANKS]
            for chunk in range(RANKS // 8):

                @pl.when(count > chunk * 8)
                def _():
                    top = held_ref[0:8, :]
                    low = held_ref[8:10, :]
                    for group in range(8 // CHAINS):
                        news = []
                        for i in range(CHAINS):
                            rank = chunk * 8 + group * CHAINS + i
                            spot = side * RANKS + rank
                            slot = asked_ref[src, rank]
                            base = pl.multiple_of((slot >> 7) << 7, 128)
                            at = slot & 127
                            turn = (slot - spot) & 127
                            a = jnp.where(lane8 == at, pltpu.roll(top, turn, 1), 0.0)
                            b = jnp.where(lane2 == at, pltpu.roll(low, turn, 1), 0.0)
                            news.append((base, a, b))
                        olds = [
                            (ref[0:8, pl.ds(base, 128)], ref[8:10, pl.ds(base, 128)])
                            for ref, (base, a, b) in zip(totals, news)
                        ]
                        for ref, (base, a, b), (old_a, old_b) in zip(totals, news, olds):
                            ref[0:8, pl.ds(base, 128)] = old_a + a
                            ref[8:10, pl.ds(base, 128)] = old_b + b

        return carry

    lax.fori_loop(0, DEVS // 2, pair, 0)

    def close(i, carry):
        at = pl.ds(pl.multiple_of(i * width, width), width)
        total = out_ref[:, at]
        for ref in more:
            total = total + ref[:, at]
        out_ref[:, at] = total
        return carry

    lax.fori_loop(0, out_ref.shape[1] // width, close, 0)


def render_kernel(
    wire_ref, owner_ref, rank_ref, target_ref, image_ref, out_ref,
    hot_ref, left_ref, value_ref, fall_ref, flow_ref, sum_ref, keep_ref, reach_ref, behind_ref,
    shade_ref, column_ref, picture_ref, across_ref, tilt_ref, grad_ref, spread_ref,
):
    for c in range(WIRE):
        block = wire_ref[pl.ds(c, DEVS, stride=WIRE), :].T
        parts = split(block, 3)
        left_ref[c * 128 : (c + 1) * 128, :] = jnp.concatenate(parts, axis=1)
    rank_of = iota((RANKS, 256), 0).astype(F32)

    def fetch(n, carry):
        at = pl.ds(pl.multiple_of(n * 256, 256), 256)
        owner = jnp.concatenate([owner_ref[pl.ds(2 * n, 1), :], owner_ref[pl.ds(2 * n + 1, 1), :]], axis=1)
        rank = jnp.concatenate([rank_ref[pl.ds(2 * n, 1), :], rank_ref[pl.ds(2 * n + 1, 1), :]], axis=1)
        hot = onehot_rows(owner, DEVS).astype(F32).astype(BF16)
        hot_ref[:, at] = hot
        mine = rank_of == rank
        found = dot(left_ref[...], jnp.concatenate([hot, hot, hot], axis=0))
        for c in range(WIRE):
            for h in range(2):
                block = found[c * 128 + h * RANKS : c * 128 + (h + 1) * RANKS]
                got = jnp.sum(jnp.where(mine, block, 0.0), axis=0, keepdims=True)
                v = c + WIRE * h
                value_ref[v, pl.ds(2 * n, 1), :] = got[:, :SEGS]
                value_ref[v, pl.ds(2 * n + 1, 1), :] = got[:, SEGS:]
        return carry

    lax.fori_loop(0, ROWS // 2, fetch, 0)

    flat = jnp.concatenate([target_ref[ch] for ch in range(4)] + [jnp.zeros((112, 256), F32)], axis=0)
    column_ref[...] = jnp.concatenate([flat[:, :128].T, flat[:, 128:].T], axis=0)
    picture_ref[...] = jnp.zeros((256, 128), F32)
    earlier = (iota((128, 128), 0) < iota((128, 128), 1)).astype(F32).astype(BF16)
    later = (iota((128, 128), 0) > iota((128, 128), 1)).astype(F32).astype(BF16)
    ones = jnp.ones((256, 128), BF16)
    earlier = jnp.concatenate([earlier, earlier, earlier], axis=0)
    later = jnp.concatenate([later, later], axis=0)
    pixel_x = iota((16, SEGS), 0).astype(F32) + 0.5

    def tile(t, carry):
        first = t * STEPS
        for k in range(STEPS):
            value = lambda v: value_ref[v, pl.ds(first + k, 1), :]
            offset_x = pixel_x - value(0)
            across_ref[k] = (-0.5 * LOG2E) * value(2) * offset_x * offset_x
            tilt_ref[k] = -LOG2E * value(3) * offset_x

        def forward(n, carry):
            for half in range(2):
                y = 2 * n + half
                pixel_y = y.astype(F32) + 0.5
                keep = jnp.ones((16, SEGS), F32)
                sums = [jnp.zeros((16, SEGS), F32) for _ in range(4)]
                at = pl.ds(pl.multiple_of(y * 16, 16), 16)
                for k in range(STEPS):
                    value = lambda v: value_ref[v, pl.ds(first + k, 1), :]
                    offset_y = pixel_y - value(1)
                    down = (-0.5 * LOG2E) * value(4) * offset_y * offset_y
                    fall = jnp.exp2(across_ref[k] + down + tilt_ref[k] * offset_y)
                    flow = fall * keep
                    weight = value(5) * flow
                    keep = keep - weight
                    for ch in range(4):
                        sums[ch] = sums[ch] + value(6 + ch) * weight
                    fall_ref[k, at, :] = fall
                    flow_ref[k, at, :] = flow
                keep_ref[at, :] = keep
                for ch in range(4):
                    sum_ref[ch, at, :] = sums[ch]
            return carry

        lax.fori_loop(0, 8, forward, 0)

        keep = keep_ref[...]
        logs = jnp.concatenate(split(jnp.log(keep), 3), axis=1)
        reach = jnp.exp(dot(logs, earlier))
        reach_ref[...] = reach
        spent = jnp.zeros((256, SEGS), F32)
        for ch in range(4):
            part = sum_ref[ch] * reach
            rendered = dot(jnp.concatenate(split(part, 2), axis=1), ones)
            here = iota((256, 128), 1) == ch * TILES + t
            wanted = jnp.sum(jnp.where(here, column_ref[...], 0.0), axis=1, keepdims=True)
            shade = 2.0 * (rendered - wanted)
            picture_ref[...] = jnp.where(here, rendered, picture_ref[...])
            shade_ref[ch] = shade
            spent = spent + shade * part
        rest = dot(jnp.concatenate(split(spent, 2), axis=1), later)
        behind_ref[...] = rest / (reach * keep)

        for k in reversed(range(STEPS)):
            value = lambda v: value_ref[v, pl.ds(first + k, 1), :]
            mean_y = jnp.broadcast_to(value(1), (8, SEGS))
            opacity = jnp.broadcast_to(value(5), (8, SEGS))
            colours = [jnp.broadcast_to(value(6 + ch), (8, SEGS)) for ch in range(4)]

            def backward(n, sums):
                zero, one, two, tints = sums
                zero, one, two, tints = list(zero), list(one), list(two), list(tints)
                for quarter in range(2):
                    y = 2 * n + quarter
                    offset_y = y.astype(F32) + 0.5 - mean_y
                    for half in range(2):
                        at = pl.ds(pl.multiple_of(y * 16 + half * 8, 8), 8)
                        shades = [shade_ref[ch, at, :] for ch in range(4)]
                        flow = flow_ref[k, at, :] * reach_ref[at, :]
                        lit = (shades[0] * colours[0] + shades[1] * colours[1]) + (
                            shades[2] * colours[2] + shades[3] * colours[3]
                        )
                        behind = behind_ref[at, :]
                        gap = lit - behind
                        behind_ref[at, :] = behind + opacity * fall_ref[k, at, :] * gap
                        grad = flow * gap
                        slope = grad * offset_y
                        zero[half] = zero[half] + grad
                        one[half] = one[half] + slope
                        two[half] = two[half] + slope * offset_y
                        for ch in range(4):
                            tints[ch] = tints[ch] + flow * shades[ch]
                return (tuple(zero), tuple(one), tuple(two), tuple(tints))

            blank = jnp.zeros((8, SEGS), F32)
            zero, one, two, tints = lax.fori_loop(
                0, 8, backward, ((blank,) * 2, (blank,) * 2, (blank,) * 2, (blank,) * 4)
            )
            total = lambda x: jnp.sum(x, axis=0, keepdims=True)
            offset_x = pixel_x - value(0)
            near, far = offset_x[:8], offset_x[8:]
            sum_0 = total(zero[0] + zero[1])
            slope_x = (near * zero[0], far * zero[1])
            sum_x = total(slope_x[0] + slope_x[1])
            sum_xx = total(near * slope_x[0] + far * slope_x[1])
            sum_y = total(one[0] + one[1])
            sum_xy = total(near * one[0] + far * one[1])
            sum_yy = total(two[0] + two[1])
            opacity = value(5)
            grads = [
                opacity * (value(2) * sum_x + value(3) * sum_y),
                opacity * (value(4) * sum_y + value(3) * sum_x),
                -0.5 * opacity * sum_xx,
                -opacity * sum_xy,
                -0.5 * opacity * sum_yy,
                sum_0,
            ] + [opacity * total(tint) for tint in tints]
            for v in range(10):
                grad_ref[v, pl.ds(first + k, 1), :] = grads[v]
        return carry

    lax.fori_loop(0, TILES, tile, 0)

    picture = picture_ref[...]
    picture = jnp.concatenate([picture[:128].T, picture[128:].T], axis=1)
    for ch in range(4):
        image_ref[ch] = picture[ch * TILES : (ch + 1) * TILES, :]

    spread_ref[...] = jnp.zeros((WIRE * 128, DEVS), F32)

    def spread(n, carry):
        at = pl.ds(pl.multiple_of(n * 256, 256), 256)
        rank = jnp.concatenate([rank_ref[pl.ds(2 * n, 1), :], rank_ref[pl.ds(2 * n + 1, 1), :]], axis=1)
        mine = rank_of == rank
        hot = hot_ref[:, at]
        rows = []
        for c in range(WIRE):
            for h in range(2):
                v = c + WIRE * h
                grad = jnp.concatenate(
                    [grad_ref[v, pl.ds(2 * n, 1), :], grad_ref[v, pl.ds(2 * n + 1, 1), :]], axis=1
                )
                rows.append(jnp.where(mine, grad, 0.0))
        heads, tails = split(jnp.concatenate(rows, axis=0), 2)
        spread_ref[...] += dot_nt(
            jnp.concatenate([heads, tails], axis=1), jnp.concatenate([hot, hot], axis=1)
        )
        return carry

    lax.fori_loop(0, ROWS // 2, spread, 0)
    for c in range(WIRE):
        out_ref[pl.ds(c, DEVS, stride=WIRE), :] = spread_ref[c * 128 : (c + 1) * 128, :].T


def vmem():
    return pl.BlockSpec(memory_space=pltpu.VMEM)


def smem():
    return pl.BlockSpec(memory_space=pltpu.SMEM)


def call(kernel, name, in_specs, outs, scratch, limit):
    return pl.pallas_call(
        kernel,
        name=name,
        out_shape=outs,
        in_specs=in_specs,
        out_specs=jax.tree.map(lambda _: vmem(), outs),
        scratch_shapes=scratch,
        compiler_params=pltpu.CompilerParams(vmem_limit_bytes=limit),
    )


def exchange(x):
    width = x.shape[0] * x.shape[1] // DEVS
    moved = lax.all_to_all(x.reshape(DEVS, 1, width), AXES, split_axis=0, concat_axis=0, tiled=True)
    return moved.reshape(x.shape)


def body(splat_params, list_owner, list_slot, list_length, target):
    shape = jax.ShapeDtypeStruct
    wire = shape((DEVS * WIRE, 128), F32)
    route = call(
        route_kernel, "route", [smem(), vmem(), vmem()],
        (shape((DEVS, 128), jnp.int32), shape((ROWS, SEGS), F32), shape((ROWS, SEGS), F32)), [], 32 << 20,
    )
    request, owners, ranks = route(list_length, list_owner.reshape(ROWS, SEGS), list_slot)
    asked = exchange(request)
    gather = call(gather_kernel, "gather", [smem(), vmem()], wire, [pltpu.VMEM((16, 128), F32)], 32 << 20)
    replies = exchange(gather(asked, splat_params))
    field = pltpu.VMEM((256, SEGS), F32)
    deep = pltpu.VMEM((STEPS, 256, SEGS), F32)
    render = call(
        render_kernel, "render", [vmem()] * 4, (shape(target.shape, F32), wire),
        [
            pltpu.VMEM((DEVS, ROWS * SEGS), BF16), pltpu.VMEM((WIRE * 128, 384), BF16),
            pltpu.VMEM((10, ROWS, SEGS), F32), deep, deep, pltpu.VMEM((4, 256, SEGS), F32), field, field, field,
            pltpu.VMEM((4, 256, SEGS), F32), field, field,
            pltpu.VMEM((STEPS, 16, SEGS), F32), pltpu.VMEM((STEPS, 16, SEGS), F32),
            pltpu.VMEM((10, ROWS, SEGS), F32), pltpu.VMEM((WIRE * 128, DEVS), F32),
        ],
        40 << 20,
    )
    images, outgoing = render(replies, owners, ranks, target)
    incoming = exchange(outgoing)
    scatter = call(
        scatter_kernel, "scatter", [smem(), vmem()], shape(splat_params.shape, F32),
        [pltpu.VMEM((16, 128), F32)] + [pltpu.VMEM(splat_params.shape, F32)] * (CHAINS - 1), 48 << 20,
    )
    return (images, scatter(asked, incoming))


def solution(mesh):
    in_specs = (
        P(None, AXES),
        P(AXES, None, None),
        P(AXES, None),
        P(AXES),
        P(None, AXES, None),
    )
    out_specs = (P(None, AXES, None), P(None, AXES))
    return jax.shard_map(body, mesh=mesh, in_specs=in_specs, out_specs=out_specs, check_vma=False)
```

time: 454 us -> 234 us (0.52)
  local copies, waits for them, and re-layouts: 260 us -> 4.28 us
  Pallas kernels: 0 us -> 175 us
  other arithmetic: 83 us -> 0 us
  matrix products: 38.7 us -> 0 us
  blocking collectives: 32.1 us -> 53.7 us
  starting transfers between devices: 21.3 us -> 0 us
  waiting for transfers between devices: 11.5 us -> 0 us
  loops' own time: 4.97 us -> 0 us
    pallas_call x0 -> x4, Pallas kernels: none -> 175 us  [the longest x1 75.5 us: body(): return (images, scatter(asked, incoming))]
    gather x18 -> x0, local copies, waits for them, and re-layouts: 148 us -> none  [the longest x1 44 us: body(): fetched = replies[:, owners, slot_rank].reshape(10, tile_count, list_count)]
    unnamed x25 -> x10, local copies, waits for them, and re-layouts: 70.9 us -> 4.28 us
    scatter-add x1 -> x0, other arithmetic: 64.3 us -> none  [body(): jnp.zeros(splat_params.shape, jnp.float32).at[:, asked_slots[0]]]
    dot_general x72 -> x0, matrix products: 38.7 us -> none  [the longest x12 10.4 us: backward(): jnp.dot(spent_sum, inclusive, precision=precise)]
    all_to_all x1 -> x3, blocking collectives: 32.1 us -> 53.7 us  [exchange(): lax.all_to_all(x.reshape(DEVS, 1, width), AXES, split_axis=0, concat_axis...]
    all_to_all x2 -> x0, starting transfers between devices: 21.3 us -> none  [the longest x1 11.5 us: body(): lax.all_to_all(requests, ('row', 'col'), split_axis=0, concat_axis=0, til...]
    scatter x1 -> x0, local copies, waits for them, and re-layouts: 15.5 us -> none  [body(): slot_rank = jnp.zeros((entries,), jnp.int32).at[sort_order].set(position)]
  transfers between devices with their start and end apart: 2 -> 0, of which waited for: 1 -> 0; matrix products, arithmetic and copies ran while one was open for 4% -> 0% of each run, Pallas kernels for 0% -> 0%
where the time goes in v1:
time: 234 us
  Pallas kernels  175 us (75%)
  blocking collectives  53.7 us (23%)
  local copies, waits for them, and re-layouts  4.28 us (2%)
    pallas_call x1, Pallas kernels, body(): return (images, scatter(asked, incoming))  75.5 us
    pallas_call x1, Pallas kernels, body(): replies = exchange(gather(asked, splat_params))  74 us
    all_to_all x3, blocking collectives, exchange(): lax.all_to_all(x.reshape(DEVS, 1, width), AXES, split_axis=0, concat_axis...  53.7 us
    pallas_call x1, Pallas kernels, body(): images, outgoing = render(replies, owners, ranks, target)  22.9 us

profile of v1, /device:TPU:1, one launch (start us, length us, event | category | flops | bytes accessed | tf_op | source)
XLA Modules:
  0.0 233.6 jit_solution(8942626808594633977)
XLA Ops:
  0.6 0.0 copy-start.1
  0.6 0.0 copy-start.2
  0.7 0.7 copy-done.2
  1.4 0.0 copy-start.3
  1.4 0.7 copy-done.3
  2.1 0.0 copy-start.4
  2.1 0.7 copy-done.4
  2.7 2.6 %route.1 = (s32[128,128]{1,0:T(8,128)S(1)}, f32[32,128]{1,0:T(8,128)S(1)}, f32[32,128]{1,0:T(8,128)S(1)}) custom-call(s32[4]{0:T(128)S(1)} %copy-done.4, s32[32,128]{1,0:T(8,128)S(1)} %bitcast.16, s32[4,1024]{1,0:T(4,128)S(1)} %copy-done.3), custom_call_target="tpu_custom_call" | custom-call | tf_op jit(solution)/shard_map/route/pallas_call | solution.py:422
  5.3 20.9 %all_to_all.15 = s32[128,1,128]{2,1,0:T(1,128)S(1)} all-to-all(s32[128,1,128]{2,1,0:T(1,128)S(1)} %bitcast.15), channel_id=1, replica_groups=mesh['row'=4,'col'=32] {'row','col'}, dimensions={0} | all-to-all | bytes 131072 | tf_op jit(solution)/shard_map/all_to_all | solution.py:411
  26.2 0.0 copy-start
  26.2 2.2 copy-done
  28.4 74.0 %gather.1 = f32[640,128]{1,0:T(8,128)S(1)} custom-call(s32[128,128]{1,0:T(8,128)S(1)} %bitcast.12, f32[10,65536]{1,0:T(8,128)S(1)} %copy-done), custom_call_target="tpu_custom_call" | custom-call | tf_op jit(solution)/shard_map/gather/pallas_call | solution.py:425
  102.4 16.9 %all_to_all.16 = f32[128,1,640]{2,1,0:T(1,128)S(1)} all-to-all(f32[128,1,640]{2,1,0:T(1,128)S(1)} %bitcast.10), channel_id=1, replica_groups=mesh['row'=4,'col'=32] {'row','col'}, dimensions={0} | all-to-all | bytes 655360 | tf_op jit(solution)/shard_map/all_to_all | solution.py:411
  119.2 0.0 copy-done.1
  119.2 22.9 %render.1 = (f32[4,4,256]{2,1,0:T(4,128)}, f32[640,128]{1,0:T(8,128)S(1)}) custom-call(f32[640,128]{1,0:T(8,128)S(1)} %bitcast.11, f32[32,128]{1,0:T(8,128)S(1)} %get-tuple-element.8.owner_ref, f32[32,128]{1,0:T(8,128)S(1)} %get-tuple-element.9.rank_ref, f32[4,4,256]{2,1,0:T(4,128)S(1)} %copy-done.1), custom_call_target="tpu_custom_call" | custom-call | tf_op jit(solution)/shard_map/render/pallas_call | solution.py:439
  142.2 15.9 %all_to_all.17 = f32[128,1,640]{2,1,0:T(1,128)S(1)} all-to-all(f32[128,1,640]{2,1,0:T(1,128)S(1)} %bitcast.14), channel_id=1, replica_groups=mesh['row'=4,'col'=32] {'row','col'}, dimensions={0} | all-to-all | bytes 655360 | tf_op jit(solution)/shard_map/all_to_all | solution.py:411
  158.1 75.5 %scatter.1 = f32[10,65536]{1,0:T(8,128)} custom-call(s32[128,128]{1,0:T(8,128)S(1)} %bitcast.13, f32[640,128]{1,0:T(8,128)S(1)} %bitcast.9), custom_call_target="tpu_custom_call" | custom-call | tf_op jit(solution)/shard_map/scatter/pallas_call | solution.py:445
Async XLA Ops:
  0.6 118.6 %copy-start.1 = (f32[4,4,256]{2,1,0:T(4,128)S(1)}, f32[4,4,256]{2,1,0:T(4,128)}, u32[]{:S(2)}) copy-start(f32[4,4,256]{2,1,0:T(4,128)} %target_ref.1) | copy-start | bytes 49156
  0.6 0.7 copy-start.2
  1.4 0.7 copy-start.3
  2.1 0.7 copy-start.4
  26.2 2.2 copy-start
